TPU v7x, 256 devices: a whole 4x4x8 slice. The times are simulated.
256 devices in a mesh: samples: 32 (over x, z_lo, core), variants: 8 (over y, z_hi).
Axes of the slice: x: 4, y: 4, z: 8 (z_hi: 2, z_lo: 4; z = z_hi * 4 + z_lo), core: 2. Of those that a mesh axis runs over, the one named last changes fastest.
Arguments:
- dosage: bfloat16 [65536, 16384], P('samples', 'variants'), may hold values from 0 to 2, as said below
- sketch: bfloat16 [16384, 256], P(('variants', 'samples')), may hold values from -0.046875 to 0.046875
Outputs:
- basis: float32 [65536, 256], P(('samples', 'variants'))
- loadings: float32 [16384, 256], P(('variants', 'samples'))
Inputs may be any that keep to these rules, and one draw needn't show every extreme that they name: `dosage`: imputed allele dosages.
All inputs are finite; a program needn't handle non-finite values.
Results may differ from a plain program's by a relative error of at most 0.0032.
Values may be sent and summed in bfloat16 or wider, within the bound.
A program may use at most 64 MiB of HBM per device.

v0:
```python
import math

import jax
import jax.numpy as jnp
from jax import lax
from jax.sharding import PartitionSpec as P


def local(dosage, sketch):
    rows, cols = dosage.shape
    count = rows * lax.axis_size("samples")
    local_total = jnp.sum(dosage.astype(jnp.float32), axis=0)
    mean = lax.psum(local_total, "samples") / count
    centered = dosage.astype(jnp.float32) - mean
    spread = lax.psum(jnp.sum(centered * centered, axis=0), "samples")
    variance = spread / count
    inv_sd = lax.rsqrt(variance + 1e-05)
    scale = inv_sd
    centre = mean
    weights = (
        scale[:, None] * lax.all_gather(sketch, "samples", axis=0, tiled=True).astype(jnp.float32)
    ).astype(jnp.bfloat16)
    columns = dosage
    summed = jnp.dot(columns, weights, preferred_element_type=jnp.float32)
    shift = jnp.dot(centre[None, :], weights.astype(jnp.float32), precision=lax.Precision.HIGHEST)
    summed, shift = (summed, shift)
    term = summed - shift
    sketch_part = lax.psum_scatter(term, "variants", scatter_dimension=0, tiled=True)
    local_gram = jnp.dot(sketch_part.T, sketch_part, precision=lax.Precision.HIGHEST)
    gram = lax.psum(local_gram, ("samples", "variants")) / count
    lower = jnp.linalg.cholesky(gram)
    basis_part = lax.linalg.triangular_solve(
        lower, sketch_part, left_side=False, lower=True, transpose_a=True
    )
    basis_half = lax.all_gather(basis_part.astype(jnp.bfloat16), "variants", axis=0, tiled=True)
    column_sums = jnp.sum(basis_half.astype(jnp.float32), axis=0)
    root = math.sqrt(count)
    columns = dosage
    product = lax.dot_general(
        columns, basis_half, (((0,), (0,)), ((), ())), preferred_element_type=jnp.float32
    )
    centre = mean
    scale = inv_sd / root
    loadings = lax.psum_scatter(
        scale[:, None] * (product - centre[:, None] * column_sums[None, :]),
        "samples",
        scatter_dimension=0,
        tiled=True,
    )
    return (basis_part, loadings)


def solution(mesh):
    in_specs = (P("samples", "variants"), P(("variants", "samples"), None))
    out_specs = (P(("samples", "variants"), None), P(("variants", "samples"), None))
    return jax.shard_map(local, mesh=mesh, in_specs=in_specs, out_specs=out_specs, check_vma=False)
```

profile of v0, /device:TPU:1, one launch (start us, length us, event | category | flops | bytes accessed | tf_op | source)
XLA Modules:
  0.0 796.5 jit_solution(8534592585396762690)
XLA Ops:
  7.9 4.7 convert_reduce_fusion
  12.7 71.3 %psum.21 = f32[2048]{0:T(1024)S(1)} all-reduce(f32[2048]{0:T(1024)S(1)} %convert_reduce_fusion), channel_id=1, replica_groups=mesh['samples'=32,'variants'=8] {'samples'}, use_global_device_ids=true, to_apply=%region_1.0 | all-reduce | flops 2048 | bytes 16384 | tf_op jit(solution)/shard_map/psum | solution.py:13
  84.0 5.6 fusion.1
  89.6 72.7 %psum.22 = f32[2048]{0:T(1024)S(1)} all-reduce(f32[2048]{0:T(1024)S(1)} %fusion.1), channel_id=1, replica_groups=mesh['samples'=32,'variants'=8] {'samples'}, use_global_device_ids=true, to_apply=%region_3.0 | all-reduce | flops 2048 | bytes 16384 | tf_op jit(solution)/shard_map/psum | solution.py:15
  162.3 1.9 fusion.5
  164.3 7.8 fusion.4
  172.2 92.0 %reduce-scatter.5.cloned.1.call-done = f32[256,256]{0,1:T(8,128)} async-done(((f32[2048,256]{0,1:T(8,128)}), f32[256,256]{0,1:T(8,128)}) %reduce-scatter.5.cloned.1.call-update) | async-done | bytes 262160 | tf_op jit(solution)/shard_map/reduce_scatter | solution.py:28
  264.1 2.1 fusion.16
  266.6 250.4 %all-reduce.3.cloned.1.call-done = f32[256,256]{0,1:T(8,128)} async-done(((f32[256,256]{0,1:T(8,128)}), f32[256,256]{0,1:T(8,128)}) %all-reduce.3.cloned.1.call-update) | async-done | bytes 262160 | tf_op jit(solution)/shard_map/psum | solution.py:30
  517.0 1.0 broadcast_multiply_fusion
  518.1 1.0 fusion.6
  519.1 11.7 %cholesky.50 = f32[128,128]{1,0:T(8,128)S(1)} custom-call(f32[128,128]{1,0:T(8,128)S(1)} %cholesky.118), custom_call_target="Cholesky" | custom-call | tf_op jit(solution)/shard_map/jit(cholesky)/cholesky | solution.py:31
  530.9 9.8 %custom-call.14 = f32[1,128,128]{1,2,0:T(8,128)S(1)} custom-call(f32[1,128,128]{2,1,0:T(8,128)S(1)} %get-tuple-element.27), custom_call_target="InvertDiagBlocksLowerTriangular" | custom-call | tf_op jit(solution)/shard_map/jit(cholesky)/cholesky | solution.py:31
  541.2 11.7 %cholesky.105 = f32[128,128]{1,0:T(8,128)S(1)} custom-call(f32[128,128]{1,0:T(8,128)S(1)} %convolution_subtract_fusion.2), custom_call_target="Cholesky" | custom-call | tf_op jit(solution)/shard_map/jit(cholesky)/cholesky | solution.py:31
  555.1 4.3 while.1
  555.9 1.4 bitcast_dynamic-update-slice_fusion.2
  558.0 1.4 bitcast_dynamic-update-slice_fusion.2
  559.4 19.7 %custom-call.15 = f32[2,128,128]{1,2,0:T(8,128)S(1)} custom-call(f32[2,128,128]{2,1,0:T(8,128)S(1)} %get-tuple-element.9), custom_call_target="InvertDiagBlocksLowerTriangular" | custom-call | tf_op jit(solution)/shard_map/triangular_solve | solution.py:32
  580.8 60.5 %all-gather.5.cloned.1.call-done = bf16[2048,256]{0,1:T(8,128)(2,1)} async-done(((bf16[256,256]{0,1:T(8,128)(2,1)}), bf16[2048,256]{0,1:T(8,128)(2,1)}) %all-gather.5.cloned.1.call-update) | async-done | bytes 1048592 | tf_op jit(solution)/shard_map/all_gather | solution.py:35
  641.3 1.4 convert_reduce_fusion.1
  642.7 6.1 fusion.3
  648.8 1.9 copy.13
  650.7 0.8 copy.10
  651.6 138.4 %reduce-scatter.7.cloned.1.call-done = f32[64,256]{1,0:T(8,128)} async-done(((f32[2048,256]{1,0:T(8,128)}), f32[64,256]{1,0:T(8,128)}) %reduce-scatter.7.cloned.1.call-update) | async-done | bytes 65552
  (36 shorter events, 5.5 us)
Async XLA Ops:
  7.2 155.2 %all-gather.3.cloned.1.call-start = ((), (), s32[]{:S(2)}) async-start(), calls=%async_computation.2 | async-start | bytes 1081344 | tf_op jit(solution)/shard_map/all_gather | solution.py:21
  7.9 256.2 %reduce-scatter.5.cloned.1.call-start = ((), (), s32[]{:S(2)}) async-start(), calls=%async_computation.3 | async-start | bytes 2359296 | tf_op jit(solution)/shard_map/reduce_scatter | solution.py:28
  172.1 344.9 %all-reduce.3.cloned.1.call-start = ((), (), s32[]{:S(2)}) async-start(), calls=%async_computation.4 | async-start | bytes 524288 | tf_op jit(solution)/shard_map/psum | solution.py:30
  266.3 375.0 %all-gather.5.cloned.1.call-start = ((), (), s32[]{:S(2)}) async-start(), calls=%async_computation.5 | async-start | bytes 1179648 | tf_op jit(solution)/shard_map/all_gather | solution.py:35
  518.0 61.1 %copy-start = (f32[256,256]{0,1:T(8,128)S(1)}, f32[256,256]{0,1:T(8,128)}, u32[]{:S(2)}) copy-start(f32[256,256]{0,1:T(8,128)} %reduce-scatter.5.cloned.1.call-done) | copy-start | bytes 786436
  580.7 209.2 %reduce-scatter.7.cloned.1.call-start = ((), (), s32[]{:S(2)}) async-start(), calls=%async_computation.6 | async-start | bytes 2162688
Sparse Core Ops, SparseCore 0:
  9.9 63.0 all-gather.2
  172.2 91.8 reduce-scatter.4
  271.1 245.9 all-reduce.2
  580.9 60.3 all-gather.4
  650.8 139.0 reduce-scatter.6
where the time goes:
time: 801 us; the launch traced here: 796 us
  waiting for transfers between devices  542 us (68%)
  blocking collectives  144 us (18%)
  other arithmetic  68.2 us (9%)
  matrix products  19.4 us (2%)
  between operations  15.3 us (2%)
    psum x1, waiting for transfers between devices, local(): gram = lax.psum(local_gram, ('samples', 'variants')) / count  250 us
    unnamed x6, waiting for transfers between devices  139 us
    reduce_scatter x1, waiting for transfers between devices, local(): lax.psum_scatter(term, 'variants', scatter_dimension=0, tiled=True)  92 us
    psum x1, blocking collectives, local(): spread = lax.psum(jnp.sum(centered * centered, axis=0), 'samples')  72.7 us
    psum x1, blocking collectives, local(): mean = lax.psum(local_total, 'samples') / count  71.3 us
    all_gather x1, waiting for transfers between devices, local(): lax.all_gather(basis_part.astype(jnp.bfloat16), 'variants', axis=0, tiled...  60.5 us
    another operation x6, other arithmetic, local(): lower = jnp.linalg.cholesky(gram)  34 us
    another operation x4, other arithmetic, local(): lax.linalg.triangular_solve(lower, sketch_part, left_side=False, lower=Tr...  19.7 us
  transfers between devices with their start and end apart: 5, of which 4 were waited for; matrix products, arithmetic and copies ran while one was open for 1% of the time, Pallas kernels for 0%

commit v1 on v0

v1 whole, which is shorter than its diff:
```python
import functools
import math

import jax
import jax.numpy as jnp
from jax import lax
from jax.experimental import pallas as pl
from jax.experimental.pallas import tpu as pltpu
from jax.sharding import PartitionSpec as P

MESH = pl.DeviceIdType.MESH
HIGHEST = lax.Precision.HIGHEST
F32 = jnp.float32
BF16 = jnp.bfloat16
NX, NZL, NC, NY, NZH = 4, 4, 2, 4, 2
EPS = 1e-05


def coords():
    s = lax.axis_index("samples")
    v = lax.axis_index("variants")
    return s // 8, (s // 2) % 4, s % 2, v // 2, v % 2


def peer(dx=0, dzl=0, dc=0, dy=0, dzh=0):
    x, zl, c, y, zh = coords()
    x = (x + dx) % NX
    zl = (zl + dzl) % NZL
    c = (c + dc) % NC
    y = (y + dy) % NY
    zh = (zh + dzh) % NZH
    return ((x * NZL + zl) * NC + c, y * NZH + zh)


def loop(low, high, body):
    def step(k, carry):
        body(k)
        return carry

    lax.fori_loop(low, high, step, 0)


def comm_kernel(
    count, x_hbm, sk_ref, g_out, p_out, t_out,
    X, skbuf, W, st, st_c, st_x, st_z, Pp, yA, yB, zsend, zrecv,
    PG, TT, trecv, TM, tx, TX, tz, tfin, gbuf, grecv, gxy, gz, gfin,
    x_sem, c_ssem, c_rsem, sk_ssem, sk_rsem, st_ssem, st_rsem, y_ssem, y_rsem,
    z_ssem, z_rsem, g_ssem, g_rsem, t_ssem, t_rsem,
):
    x, zl, c, y, zh = coords()
    v = y * NZH + zh
    vz = y * NZH + (1 - zh)
    xz = x * NZL + zl
    xy = x * NY + y
    z = zh * NZL + zl
    blocks, rows, cols = X.shape
    local_count = blocks * rows

    def load(i):
        return pltpu.make_async_copy(x_hbm.at[pl.ds(i * rows, rows)], X.at[i], x_sem.at[i])

    def send(src, dst, ssem, rsem, to):
        return pltpu.make_async_remote_copy(
            src_ref=src, dst_ref=dst, send_sem=ssem, recv_sem=rsem, device_id=to, device_id_type=MESH
        )

    loop(0, blocks, lambda i: load(i).start())

    barrier = pltpu.get_barrier_semaphore()

    def greet(to):
        pl.semaphore_signal(barrier, inc=1, device_id=to, device_id_type=MESH)

    greet(peer(dc=1))
    loop(1, 16, lambda k: greet(peer(dx=k // 4, dzl=k % 4)))
    loop(0, 12, lambda k: greet(peer(dx=k // 3, dy=k % 3 + 1)))
    loop(0, 4, lambda k: greet(peer(dzl=k, dzh=1)))

    lane = 512
    pieces = cols // lane

    load(0).wait()
    pivots = []
    for h in range(pieces):

        def add_rows(r, acc, h=h):
            d = X[0, pl.ds(pl.multiple_of(r * 16, 16), 16), pl.ds(h * lane, lane)].astype(F32)
            return acc + (d[:8] + d[8:])

        acc = lax.fori_loop(0, rows // 16, add_rows, jnp.zeros((8, lane), F32), unroll=4)
        pivots.append(jnp.sum(acc, axis=0, keepdims=True) / rows)

    def spread_of(i, carry):
        out = []
        for h in range(pieces):

            def add_rows(r, acc, h=h):
                s1, s2 = acc
                d = X[i, pl.ds(pl.multiple_of(r * 16, 16), 16), pl.ds(h * lane, lane)].astype(F32) - pivots[h]
                q = d * d
                return s1 + (d[:8] + d[8:]), s2 + (q[:8] + q[8:])

            out.append(lax.fori_loop(0, rows // 16, add_rows, carry[h], unroll=4))
        return tuple(out)

    zero = jnp.zeros((8, lane), F32)
    sums = tuple((zero, zero) for _ in range(pieces))
    half = blocks // 2

    def block_sums(i, carry):
        @pl.when(i > 0)
        def _():
            load(i).wait()

        return spread_of(i, carry)

    sums = lax.fori_loop(0, half, block_sums, sums)

    pl.semaphore_wait(barrier, 32)

    def sketch_copy(k):
        return send(sk_ref, skbuf.at[xz, c], sk_ssem.at[k], sk_rsem.at[k], peer(dx=k // 4, dzl=k % 4))

    loop(1, 16, lambda k: sketch_copy(k).start())
    skbuf[xz, c] = sk_ref[...]

    sums = lax.fori_loop(half, blocks, block_sums, sums)

    for h in range(pieces):
        s1 = jnp.sum(sums[h][0], axis=0, keepdims=True)
        s2 = jnp.sum(sums[h][1], axis=0, keepdims=True)
        mean = pivots[h] + s1 / local_count
        m2 = s2 - s1 * s1 / local_count
        for q in range(lane // 128):
            g = h * (lane // 128) + q
            st[g : g + 1, :] = mean[:, q * 128 : (q + 1) * 128]
            st[16 + g : 17 + g, :] = m2[:, q * 128 : (q + 1) * 128]

    copy = send(st, st_c, c_ssem.at[0], c_rsem.at[0], peer(dc=1))
    copy.start()
    copy.wait()
    a, b = st[...], st_c[...]
    n = float(local_count)
    delta = a[:16] - b[:16]
    st_x[x, :16] = 0.5 * (a[:16] + b[:16])
    st_x[x, 16:] = a[16:] + b[16:] + (0.5 * n) * delta * delta
    n = 2.0 * n

    def merge(ref, n):
        mean = 0.25 * ((ref[0, :16] + ref[1, :16]) + (ref[2, :16] + ref[3, :16]))
        m2 = (ref[0, 16:] + ref[1, 16:]) + (ref[2, 16:] + ref[3, 16:])
        for i in range(4):
            d = ref[i, :16] - mean
            m2 = m2 + n * (d * d)
        return mean, m2

    def stat_x(k):
        return send(st_x.at[x], st_x.at[x], st_ssem.at[k], st_rsem.at[k], peer(dx=k))

    def stat_z(k):
        return send(st_z.at[zl], st_z.at[zl], st_ssem.at[4 + k], st_rsem.at[4 + k], peer(dzl=k))

    loop(1, 4, lambda k: stat_x(k).start())
    loop(1, 4, lambda k: stat_x(k).wait())
    mean, m2 = merge(st_x, n)
    n = 4.0 * n
    st_z[zl, :16] = mean
    st_z[zl, 16:] = m2
    loop(1, 4, lambda k: stat_z(k).start())

    loop(1, 16, lambda k: sketch_copy(k).wait())
    sketch_core = send(skbuf.at[:, c], skbuf.at[:, c], c_ssem.at[1], c_rsem.at[1], peer(dc=1))
    sketch_core.start()

    loop(1, 4, lambda k: stat_z(k).wait())
    mean, m2 = merge(st_z, n)
    inv_sd = lax.rsqrt(m2 / count + EPS)
    st[:16, :] = mean
    st[16:, :] = inv_sd
    columns = jnp.transpose(jnp.concatenate([mean, inv_sd, jnp.zeros((96, 128), F32)], axis=0))
    sketch_core.wait()

    shift = jnp.zeros((8, 256), F32)
    for g in range(16):
        sk = skbuf[g].reshape(128, 256).astype(F32)
        w = (columns[:, 16 + g : 17 + g] * sk).astype(BF16)
        W[g * 128 : (g + 1) * 128, :] = w
        shift = shift + jnp.sum((columns[:, g : g + 1] * w.astype(F32)).reshape(16, 8, 256), axis=0)
    shift = jnp.sum(shift, axis=0, keepdims=True)

    def project(i):
        Pp[i] = jnp.dot(X[i], W[...], preferred_element_type=F32) - shift

    def copy_a(k):
        return send(Pp.at[((y + k) % NY) * NZH + (1 - zh)], yA.at[y], y_ssem.at[k], y_rsem.at[k], peer(dy=k))

    def copy_b(k):
        return send(Pp.at[((y + k) % NY) * NZH + zh], yB.at[y], y_ssem.at[4 + k], y_rsem.at[4 + k], peer(dy=k))

    def project_a(k):
        project(((y + k) % NY) * NZH + (1 - zh))

        @pl.when(k < 4)
        def _():
            copy_a(k).start()

    def project_b(k):
        project(((y + k) % NY) * NZH + zh)

    loop(1, 5, project_a)
    loop(1, 5, project_b)

    loop(1, 4, lambda k: copy_a(k).wait())
    zsend[...] = (Pp[vz] + yA[(y + 1) % NY]) + (yA[(y + 2) % NY] + yA[(y + 3) % NY])
    z_copy = send(zsend, zrecv, z_ssem.at[0], z_rsem.at[0], peer(dzh=1))
    z_copy.start()
    loop(1, 4, lambda k: copy_b(k).start())
    loop(1, 4, lambda k: copy_b(k).wait())
    own = (Pp[v] + yB[(y + 1) % NY]) + (yB[(y + 2) % NY] + yB[(y + 3) % NY])
    z_copy.wait()
    own = own + zrecv[...]
    p_out[...] = own

    PG[v] = jnp.transpose(own).astype(BF16)

    def gather_own(k):
        return send(PG.at[v], PG.at[v], y_ssem.at[8 + k], y_rsem.at[8 + k], peer(dy=k))

    def gather_other(k):
        return send(PG.at[vz], PG.at[vz], y_ssem.at[12 + k], y_rsem.at[12 + k], peer(dy=k))

    gather_z = send(PG.at[v], PG.at[v], z_ssem.at[1], z_rsem.at[1], peer(dzh=1))
    gather_z.start()
    loop(1, 4, lambda k: gather_own(k).start())

    gram = lax.dot_general(own, own, (((0,), (0,)), ((), ())), precision=HIGHEST, preferred_element_type=F32)
    gbuf[...] = (gram / count).reshape(gbuf.shape)
    g_core = send(gbuf.at[1 - c], grecv, c_ssem.at[2], c_rsem.at[2], peer(dc=1))
    g_core.start()
    g_core.wait()
    gbuf[c] = gbuf[c] + grecv[...]
    gxy[xy] = gbuf[c, xy]

    def gram_scatter(k):
        to = ((x + k // 4) % NX) * NY + (y + k % 4) % NY
        return send(gbuf.at[c, to], gxy.at[xy], g_ssem.at[k], g_rsem.at[k], peer(dx=k // 4, dy=k % 4))

    def gram_z(k):
        return send(gz.at[z], gz.at[z], g_ssem.at[16 + k], g_rsem.at[16 + k], peer(dzh=k // 4, dzl=k % 4))

    def gram_gather(k):
        return send(gfin.at[c, xy], gfin.at[c, xy], g_ssem.at[24 + k], g_rsem.at[24 + k], peer(dx=k // 4, dy=k % 4))

    loop(1, 16, lambda k: gram_scatter(k).start())
    loop(1, 16, lambda k: gram_scatter(k).wait())
    gz[z] = jnp.sum(gxy[...], axis=0)
    loop(1, 8, lambda k: gram_z(k).start())

    gather_z.wait()
    loop(1, 4, lambda k: gather_other(k).start())

    loop(1, 8, lambda k: gram_z(k).wait())
    gfin[c, xy] = jnp.sum(gz[...], axis=0)
    loop(1, 16, lambda k: gram_gather(k).start())

    loop(1, 4, lambda k: gather_own(k).wait())

    def first_product(j):
        at = pl.ds(pl.multiple_of(j * 256, 256), 256)
        acc = jnp.zeros((256, 256), F32)
        for q in range(NY):
            i = q * NZH + zh
            acc = acc + jnp.dot(PG[i], X[i, :, at], preferred_element_type=F32)
        TT[:, at] = acc

    loop(0, cols // 256, first_product)

    loop(1, 16, lambda k: gram_gather(k).wait())
    g_back = send(gfin.at[c], gfin.at[c], c_ssem.at[3], c_rsem.at[3], peer(dc=1))
    g_back.start()

    loop(1, 4, lambda k: gather_other(k).wait())
    total = jnp.zeros((256, 128), F32)
    for i in range(8):
        part = PG[i].astype(F32)
        total = total + (part[:, :128] + part[:, 128:])
    total = jnp.sum(total, axis=1, keepdims=True)
    root = math.sqrt(count)

    def second_product(j):
        at = pl.ds(pl.multiple_of(j * 256, 256), 256)
        acc = TT[:, at]
        for q in range(NY):
            i = q * NZH + (1 - zh)
            acc = acc + jnp.dot(PG[i], X[i, :, at], preferred_element_type=F32)
        for q in range(2):
            g = 2 * j + q
            part = acc[:, q * 128 : (q + 1) * 128]
            part = (st[pl.ds(16 + g, 1), :] / root) * (part - total * st[pl.ds(g, 1), :])
            TT[:, pl.ds(pl.multiple_of(g * 128, 128), 128)] = part

    loop(0, cols // 256, second_product)
    g_back.wait()
    g_out[...] = gfin[...].reshape(256, 256)

    t_core = send(TT.at[pl.ds(pl.multiple_of((1 - c) * 128, 128), 128)], trecv, c_ssem.at[4], c_rsem.at[4], peer(dc=1))
    t_core.start()
    t_core.wait()
    mine = pl.ds(pl.multiple_of(c * 128, 128), 128)

    def merge_core(j):
        at = pl.ds(pl.multiple_of(j * 512, 512), 512)
        TM[j] = TT[mine, at] + trecv[:, at]

    loop(0, 4, merge_core)

    def t_x(k):
        return send(TM.at[(x + k) % NX], tx.at[x], t_ssem.at[k], t_rsem.at[k], peer(dx=k))

    def t_z(k):
        return send(TX.at[(zl + k) % NZL], tz.at[zl], t_ssem.at[4 + k], t_rsem.at[4 + k], peer(dzl=k))

    loop(1, 4, lambda k: t_x(k).start())
    loop(1, 4, lambda k: t_x(k).wait())
    acc = (TM[x] + tx[(x + 1) % NX]) + (tx[(x + 2) % NX] + tx[(x + 3) % NX])
    for q in range(NZL):
        TX[q] = acc[:, q * 128 : (q + 1) * 128]
    loop(1, 4, lambda k: t_z(k).start())
    loop(1, 4, lambda k: t_z(k).wait())
    tfin[mine] = (TX[zl] + tz[(zl + 1) % NZL]) + (tz[(zl + 2) % NZL] + tz[(zl + 3) % NZL])
    t_back = send(tfin.at[mine], tfin.at[mine], c_ssem.at[5], c_rsem.at[5], peer(dc=1))
    t_back.start()
    t_back.wait()
    t_out[...] = tfin[...]


def communicate(dosage, sketch, count):
    rows, cols = dosage.shape
    k = sketch.shape[1]
    vm = pltpu.VMEM
    dma = pltpu.SemaphoreType.DMA
    vmem = pl.BlockSpec(memory_space=pltpu.VMEM)
    return pl.pallas_call(
        functools.partial(comm_kernel, count),
        out_shape=(
            jax.ShapeDtypeStruct((k, k), F32),
            jax.ShapeDtypeStruct((rows // 8, k), F32),
            jax.ShapeDtypeStruct((k, 128), F32),
        ),
        in_specs=[pl.BlockSpec(memory_space=pl.ANY), vmem],
        out_specs=(vmem, vmem, vmem),
        scratch_shapes=[
            vm((8, rows // 8, cols), BF16),
            vm((16, 2, 64, k), BF16),
            vm((cols, k), BF16),
            vm((32, 128), F32),
            vm((32, 128), F32),
            vm((4, 32, 128), F32),
            vm((4, 32, 128), F32),
            vm((8, rows // 8, k), F32),
            vm((4, rows // 8, k), F32),
            vm((4, rows // 8, k), F32),
            vm((rows // 8, k), F32),
            vm((rows // 8, k), F32),
            vm((8, k, rows // 8), BF16),
            vm((k, cols), F32),
            vm((k // 2, cols), F32),
            vm((4, k // 2, cols // 4), F32),
            vm((4, k // 2, cols // 4), F32),
            vm((4, k // 2, 128), F32),
            vm((4, k // 2, 128), F32),
            vm((k, 128), F32),
            vm((2, 16, 8, k), F32),
            vm((16, 8, k), F32),
            vm((16, 8, k), F32),
            vm((8, 8, k), F32),
            vm((2, 16, 8, k), F32),
            dma((8,)),
            dma((6,)), dma((6,)),
            dma((16,)), dma((16,)),
            dma((8,)), dma((8,)),
            dma((16,)), dma((16,)),
            dma((2,)), dma((2,)),
            dma((40,)), dma((40,)),
            dma((8,)), dma((8,)),
        ],
        compiler_params=pltpu.CompilerParams(
            collective_id=0, has_side_effects=True, vmem_limit_bytes=56 * 2**20
        ),
        name="power_step",
    )(dosage, sketch)


NB = 64


def factor_kernel(g_ref, p_ref, t_ref, basis_ref, load_ref, M, Y):
    n = g_ref.shape[0]
    M[:, :n] = g_ref[...]
    row = lax.broadcasted_iota(jnp.int32, (n, n), 0)
    col = lax.broadcasted_iota(jnp.int32, (n, n), 1)
    M[:, n:] = (row == col).astype(F32)
    eye = (lax.broadcasted_iota(jnp.int32, (NB, NB), 0) == lax.broadcasted_iota(jnp.int32, (NB, NB), 1)).astype(F32)
    for b in range(n // NB):
        at = slice(b * NB, (b + 1) * NB)
        D = jnp.concatenate([M[at, at], eye], axis=1)
        for i in range(NB):
            r = lax.rsqrt(D[i : i + 1, i : i + 1])
            y = D[i : i + 1, :] * r
            Y[i : i + 1, :] = y
            if i + 1 < NB:
                D = D - (D[:, i : i + 1] * r) * y
        panel = jnp.dot(Y[:, NB:], M[at, :], precision=HIGHEST, preferred_element_type=F32)
        M[at, :] = panel
        if (b + 1) * NB < n:
            rest = slice((b + 1) * NB, n)
            M[rest, :] = M[rest, :] - lax.dot_general(
                panel[:, rest], panel, (((0,), (0,)), ((), ())), precision=HIGHEST, preferred_element_type=F32
            )
    inverse = M[:, n:]
    basis_ref[...] = lax.dot_general(
        p_ref[...], inverse, (((1,), (1,)), ((), ())), precision=HIGHEST, preferred_element_type=F32
    )
    loads = jnp.transpose(jnp.dot(inverse, t_ref[...], precision=HIGHEST, preferred_element_type=F32))
    c = lax.axis_index("samples") % NC
    load_ref[...] = jnp.where(c == 0, loads[:64], loads[64:])


def finish(gram, projected, t):
    n = gram.shape[0]
    vmem = pl.BlockSpec(memory_space=pltpu.VMEM)
    return pl.pallas_call(
        factor_kernel,
        out_shape=(
            jax.ShapeDtypeStruct(projected.shape, F32),
            jax.ShapeDtypeStruct((64, n), F32),
        ),
        in_specs=[vmem, vmem, vmem],
        out_specs=(vmem, vmem),
        scratch_shapes=[pltpu.VMEM((n, 2 * n), F32), pltpu.VMEM((NB, 2 * NB), F32)],
        compiler_params=pltpu.CompilerParams(vmem_limit_bytes=32 * 2**20),
        name="factor",
    )(gram, projected, t)


def local(dosage, sketch):
    count = dosage.shape[0] * lax.axis_size("samples")
    gram, projected, t = communicate(dosage, sketch, count)
    return finish(gram, projected, t)


def solution(mesh):
    in_specs = (P("samples", "variants"), P(("variants", "samples"), None))
    out_specs = (P(("samples", "variants"), None), P(("variants", "samples"), None))
    return jax.shard_map(local, mesh=mesh, in_specs=in_specs, out_specs=out_specs, check_vma=False)
```

time: 801 us -> 137 us (0.17)
  waiting for transfers between devices: 542 us -> 0 us
  blocking collectives: 144 us -> 0 us
  Pallas kernels: 0 us -> 133 us
  other arithmetic: 68.2 us -> 0 us
  matrix products: 19.4 us -> 0 us
  between operations: 15.3 us -> 0.65 us
    psum x1 -> x0, waiting for transfers between devices: 250 us -> none  [local(): gram = lax.psum(local_gram, ('samples', 'variants')) / count]
    psum x2 -> x0, blocking collectives: 144 us -> none  [the longest x1 72.7 us: local(): spread = lax.psum(jnp.sum(centered * centered, axis=0), 'samples')]
    unnamed x6 -> x0, waiting for transfers between devices: 139 us -> none
    pallas_call x0 -> x2, Pallas kernels: none -> 133 us  [the longest x1 108 us: communicate(): pl.pallas_call(functools.partial(comm_kernel, count), out_shape=(jax.Shap...]
    reduce_scatter x1 -> x0, waiting for transfers between devices: 92 us -> none  [local(): lax.psum_scatter(term, 'variants', scatter_dimension=0, tiled=True)]
    all_gather x2 -> x0, waiting for transfers between devices: 60.5 us -> none  [the longest x1 60.5 us: local(): lax.all_gather(basis_part.astype(jnp.bfloat16), 'variants', axis=0, tiled...]
    another operation x10 -> x0, other arithmetic: 53.8 us -> none  [the longest x6 34 us: local(): lower = jnp.linalg.cholesky(gram)]
    dot_general x4 -> x0, matrix products: 18 us -> none  [the longest x1 7.83 us: local(): summed = jnp.dot(columns, weights, preferred_element_type=jnp.float32)]
  transfers between devices with their start and end apart: 5 -> 0, of which waited for: 4 -> 0; matrix products, arithmetic and copies ran while one was open for 1% -> 0% of each run, Pallas kernels for 0% -> 0%
where the time goes in v1:
time: 137 us; the launch traced here: 136 us
  Pallas kernels  133 us (97%)
  local copies, waits for them, and re-layouts  2.8 us (2%)
    pallas_call x1, Pallas kernels, communicate(): pl.pallas_call(functools.partial(comm_kernel, count), out_shape=(jax.Shap...  108 us
    pallas_call x1, Pallas kernels, finish(): pl.pallas_call(factor_kernel, out_shape=(jax.ShapeDtypeStruct(projected.s...  24.9 us
    unnamed x6, local copies, waits for them, and re-layouts  2.8 us

profile of v1, /device:TPU:1, one launch (start us, length us, event | category | flops | bytes accessed | tf_op | source)
XLA Modules:
  0.0 136.3 jit_solution(2164527057424910300)
XLA Ops:
  0.6 108.0 %power_step.1 = (f32[256,256]{1,0:T(8,128)}, f32[256,256]{1,0:T(8,128)}, f32[256,128]{1,0:T(8,128)}) custom-call(bf16[2048,2048]{1,0:T(8,128)(2,1)} %x_hbm.1, bf16[64,256]{1,0:T(8,128)(2,1)} %sk_ref.1), custom_call_target="tpu_custom_call" | custom-call | tf_op jit(solution)/shard_map/power_step/pallas_call | solution.py:343
  108.6 0.0 copy-start
  108.6 0.9 copy-done
  109.6 0.0 copy-start.1
  109.6 0.9 copy-done.1
  110.5 0.0 copy-start.2
  110.5 0.9 copy-done.2
  111.4 24.9 %factor.1 = (f32[256,256]{1,0:T(8,128)}, f32[64,256]{1,0:T(8,128)}) custom-call(f32[256,256]{1,0:T(8,128)S(1)} %copy-done, f32[256,256]{1,0:T(8,128)S(1)} %copy-done.1, f32[256,128]{1,0:T(8,128)S(1)} %copy-done.2), custom_call_target="tpu_custom_call" | custom-call | tf_op jit(solution)/shard_map/factor/pallas_call | solution.py:432
Async XLA Ops:
  108.6 1.0 copy-start
  109.6 0.9 copy-start.1
  110.5 0.9 copy-start.2

commit v2 on v1

v2 whole, which is shorter than its diff:
```python
import functools
import math

import jax
import jax.numpy as jnp
from jax import lax
from jax.experimental import pallas as pl
from jax.experimental.pallas import tpu as pltpu
from jax.sharding import PartitionSpec as P

MESH = pl.DeviceIdType.MESH
HIGHEST = lax.Precision.HIGHEST
F32 = jnp.float32
BF16 = jnp.bfloat16
NX, NZL, NC, NY, NZH = 4, 4, 2, 4, 2
EPS = 1e-05


def coords():
    s = lax.axis_index("samples")
    v = lax.axis_index("variants")
    return s // 8, (s // 2) % 4, s % 2, v // 2, v % 2


def peer(dx=0, dzl=0, dc=0, dy=0, dzh=0):
    x, zl, c, y, zh = coords()
    x = (x + dx) % NX
    zl = (zl + dzl) % NZL
    c = (c + dc) % NC
    y = (y + dy) % NY
    zh = (zh + dzh) % NZH
    return ((x * NZL + zl) * NC + c, y * NZH + zh)


def loop(low, high, body):
    def step(k, carry):
        body(k)
        return carry

    lax.fori_loop(low, high, step, 0)


def iota(shape, axis):
    return lax.broadcasted_iota(jnp.int32, shape, axis)


NB = 64


def factor_diagonal(D, Y):
    big = (8, 128)
    n8 = NB // 8
    D = [D[8 * m : 8 * m + 8, :] for m in range(n8)]
    sub = iota(big, 0)
    for q in range(n8):
        rows = [jnp.broadcast_to(D[q][i : i + 1, :], big) for i in range(8)]
        lanes = [[jnp.broadcast_to(D[m][:, 8 * q + c : 8 * q + c + 1], big) for c in range(8)] for m in range(q, n8)]
        a = [[jnp.broadcast_to(lanes[0][c][i : i + 1, :], big) if c <= i else None for c in range(8)] for i in range(8)]
        r, l, y, z = [None] * 8, [[None] * 8 for _ in range(8)], [None] * 8, [None] * 8
        for i in range(8):
            r[i] = lax.rsqrt(a[i][i])
            for k in range(i + 1, 8):
                l[k][i] = a[k][i] * r[i]
            for k in range(i + 1, 8):
                for c in range(i + 1, k + 1):
                    a[k][c] = a[k][c] - l[k][i] * l[c][i]
            y[i] = rows[i] * r[i]
            for k in range(i + 1, 8):
                rows[k] = rows[k] - l[k][i] * y[i]
        out = y[0]
        for i in range(1, 8):
            out = jnp.where(sub == i, y[i], out)
        Y[8 * q : 8 * q + 8, :] = out
        for i in range(7, -1, -1):
            acc = y[i]
            for k in range(i + 1, 8):
                acc = acc - l[k][i] * z[k]
            z[i] = acc * r[i]
        for m in range(q + 1, n8):
            s = [lanes[m - q][k] * z[k] for k in range(8)]
            D[m] = D[m] - (((s[0] + s[1]) + (s[2] + s[3])) + ((s[4] + s[5]) + (s[6] + s[7])))


def factor_rows(M, Y, b):
    n = M.shape[0]
    at = slice(b * NB, (b + 1) * NB)
    eye = (iota((NB, NB), 0) == iota((NB, NB), 1)).astype(F32)
    factor_diagonal(jnp.concatenate([M[at, at], eye], axis=1), Y)
    panel = jnp.dot(Y[:, NB:], M[at, :], precision=HIGHEST, preferred_element_type=F32)
    M[at, :] = panel
    if (b + 1) * NB < n:
        rest = slice((b + 1) * NB, n)
        M[rest, :] = M[rest, :] - lax.dot_general(
            panel[:, rest], panel, (((0,), (0,)), ((), ())), precision=HIGHEST, preferred_element_type=F32
        )


def comm_kernel(
    count, x_hbm, sk_ref, basis_ref, load_ref,
    X, skbuf, W, st, st_c, st_x, st_z, Pp, tr, di, mg, zsend, zrecv,
    PG, TT, trecv, TM, tx, TX, tz, tfin, gbuf, grecv, gxy, gz, gfin, M, Y, own_rows,
    x_sem, c_ssem, c_rsem, sk_ssem, sk_rsem, fw_ssem, fw_rsem, st_ssem, st_rsem, y_ssem, y_rsem,
    z_ssem, z_rsem, g_ssem, g_rsem, t_ssem, t_rsem, tc_ssem, tc_rsem,
):
    x, zl, c, y, zh = coords()
    v = y * NZH + zh
    vz = y * NZH + (1 - zh)
    xz = x * NZL + zl
    xy = x * NY + y
    z = zh * NZL + zl
    blocks, rows, cols = X.shape
    local_count = blocks * rows

    def load(i):
        return pltpu.make_async_copy(x_hbm.at[pl.ds(i * rows, rows)], X.at[i], x_sem.at[i])

    def send(src, dst, ssem, rsem, to):
        return pltpu.make_async_remote_copy(
            src_ref=src, dst_ref=dst, send_sem=ssem, recv_sem=rsem, device_id=to, device_id_type=MESH
        )

    barrier = pltpu.get_barrier_semaphore()

    def greet(to):
        pl.semaphore_signal(barrier, inc=1, device_id=to, device_id_type=MESH)

    loop(0, 4, lambda k: greet(peer(dzl=k, dzh=1)))
    loop(0, 9, lambda k: greet(peer(dx=k // 3 + 1, dy=k % 3 + 1)))
    loop(0, blocks, lambda i: load(i).start())
    loop(1, 4, lambda k: greet(peer(dzl=k)))
    loop(1, 4, lambda k: greet(peer(dx=k)))
    loop(1, 4, lambda k: greet(peer(dy=k)))
    greet(peer(dc=1))

    lane = 512
    order = (1, 3, 2)
    pieces = cols // lane

    load(0).wait()
    pivots = []
    for h in range(pieces):

        def add_rows(r, acc, h=h):
            d = X[0, pl.ds(pl.multiple_of(r * 16, 16), 16), pl.ds(h * lane, lane)].astype(F32)
            return acc + (d[:8] + d[8:])

        acc = lax.fori_loop(0, rows // 16, add_rows, jnp.zeros((8, lane), F32), unroll=4)
        pivots.append(jnp.sum(acc, axis=0, keepdims=True) / rows)

    def spread_of(i, carry):
        out = []
        for h in range(pieces):

            def add_rows(r, acc, h=h):
                s1, s2 = acc
                d = X[i, pl.ds(pl.multiple_of(r * 16, 16), 16), pl.ds(h * lane, lane)].astype(F32) - pivots[h]
                q = d * d
                return s1 + (d[:8] + d[8:]), s2 + (q[:8] + q[8:])

            out.append(lax.fori_loop(0, rows // 16, add_rows, carry[h], unroll=4))
        return tuple(out)

    zero = jnp.zeros((8, lane), F32)
    sums = tuple((zero, zero) for _ in range(pieces))
    def block_sums(i, carry):
        @pl.when(i > 0)
        def _():
            load(i).wait()

        return spread_of(i, carry)

    early = 3
    sums = lax.fori_loop(0, early, block_sums, sums)

    pl.semaphore_wait(barrier, 23)

    def sketch_x(k):
        return send(sk_ref, skbuf.at[xz, c], sk_ssem.at[k], sk_rsem.at[k], peer(dx=k))

    def sketch_z(k):
        return send(sk_ref, skbuf.at[xz, c], sk_ssem.at[4 + k], sk_rsem.at[4 + k], peer(dzl=k))

    def sketch_zx(j, k):
        at = x * NZL + (zl + NZL - j) % NZL
        i = 4 * j + 4 + k
        return send(skbuf.at[at, c], skbuf.at[at, c], sk_ssem.at[i], sk_rsem.at[i], peer(dx=k))

    def sketch_core(k):
        at = pl.ds(((x + k) % NX) * NZL, NZL)
        return send(skbuf.at[at, c], skbuf.at[at, c], fw_ssem.at[k], fw_rsem.at[k], peer(dc=1))

    for k in order:
        sketch_z(k).start()
    for k in order:
        sketch_x(k).start()
    skbuf[xz, c] = sk_ref[...]

    sums = lax.fori_loop(early, blocks, block_sums, sums)

    for h in range(pieces):
        s1 = jnp.sum(sums[h][0], axis=0, keepdims=True)
        s2 = jnp.sum(sums[h][1], axis=0, keepdims=True)
        mean = pivots[h] + s1 / local_count
        m2 = s2 - s1 * s1 / local_count
        for q in range(lane // 128):
            g = h * (lane // 128) + q
            st[g : g + 1, :] = mean[:, q * 128 : (q + 1) * 128]
            st[16 + g : 17 + g, :] = m2[:, q * 128 : (q + 1) * 128]

    copy = send(st, st_c, c_ssem.at[0], c_rsem.at[0], peer(dc=1))
    copy.start()
    copy.wait()
    a, b = st[...], st_c[...]
    n = float(local_count)
    delta = a[:16] - b[:16]
    st_x[x, :16] = 0.5 * (a[:16] + b[:16])
    st_x[x, 16:] = a[16:] + b[16:] + (0.5 * n) * delta * delta
    n = 2.0 * n

    def merge(ref, n):
        mean = 0.25 * ((ref[0, :16] + ref[1, :16]) + (ref[2, :16] + ref[3, :16]))
        m2 = (ref[0, 16:] + ref[1, 16:]) + (ref[2, 16:] + ref[3, 16:])
        for i in range(4):
            d = ref[i, :16] - mean
            m2 = m2 + n * (d * d)
        return mean, m2

    def stat_x(k):
        return send(st_x.at[x], st_x.at[x], st_ssem.at[k], st_rsem.at[k], peer(dx=k))

    def stat_z(k):
        return send(st_z.at[zl], st_z.at[zl], st_ssem.at[4 + k], st_rsem.at[4 + k], peer(dzl=k))

    for k in order:
        stat_x(k).start()
    for j in order:
        sketch_z(j).wait()
        for k in order:
            sketch_zx(j, k).start()
    sketch_core(0).start()

    for k in order:
        stat_x(k).wait()
    mean, m2 = merge(st_x, n)
    n = 4.0 * n
    st_z[zl, :16] = mean
    st_z[zl, 16:] = m2
    loop(1, 4, lambda k: stat_z(k).start())

    loop(1, 4, lambda k: stat_z(k).wait())
    mean, m2 = merge(st_z, n)
    inv_sd = lax.rsqrt(m2 / count + EPS)
    st[:16, :] = mean
    st[16:, :] = inv_sd
    columns = jnp.transpose(jnp.concatenate([mean, inv_sd, jnp.zeros((96, 128), F32)], axis=0))

    for k in order:
        sketch_x(k).wait()
        for j in order:
            sketch_zx(j, k).wait()
        sketch_core(4 - k).start()
    for k in range(NX):
        sketch_core(k).wait()

    shift = jnp.zeros((8, 256), F32)
    for g in range(16):
        sk = skbuf[g].reshape(128, 256).astype(F32)
        w = (columns[:, 16 + g : 17 + g] * sk).astype(BF16)
        W[g * 128 : (g + 1) * 128, :] = w
        shift = shift + jnp.sum((columns[:, g : g + 1] * w.astype(F32)).reshape(16, 8, 256), axis=0)
    shift = jnp.sum(shift, axis=0, keepdims=True)

    def project(i):
        Pp[i] = jnp.dot(X[i], W[...], preferred_element_type=F32) - shift

    size = rows // 2
    half = size // 2

    def block(dy, p):
        return ((y + dy) % NY) * NZH + (1 - zh if p < 2 else zh)

    def part(dy, p, h):
        return Pp.at[block(dy, p), pl.ds(p % 2 * size + h * half, half)]

    def transit(p, h):
        i = 6 * p + h
        return send(part(2, p, h), tr.at[p, h], y_ssem.at[i], y_rsem.at[i], peer(dy=1 if h == 0 else 3))

    def direct(p, h):
        i = 6 * p + 2 + h
        dy = 3 if h == 0 else 1
        return send(part(dy, p, h), di.at[p, h], y_ssem.at[i], y_rsem.at[i], peer(dy=dy))

    def merged(p, h):
        i = 6 * p + 4 + h
        dy = 1 if h == 0 else 3
        return send(part(dy, p, h), mg.at[p, h], y_ssem.at[i], y_rsem.at[i], peer(dy=dy))

    def start(copy, p):
        copy(p, 0).start()
        copy(p, 1).start()

    def pass_on(p):
        for h in range(2):
            transit(p, h).wait()
            at = pl.ds(p % 2 * size + h * half, half)
            i = block(1 if h == 0 else 3, p)
            Pp[i, at] = Pp[i, at] + tr[p, h]
            merged(p, h).start()

    def arrived(p):
        for h in range(2):
            direct(p, h).wait()
            merged(p, h).wait()
        return Pp[block(0, p), pl.ds(p % 2 * size, size)] + (di[p] + mg[p]).reshape(size, -1)

    def z_copy(p):
        return send(zsend.at[p], zrecv.at[p], z_ssem.at[p], z_rsem.at[p], peer(dzh=1))

    project(block(2, 0))
    start(transit, 0)
    start(transit, 1)
    project(block(1, 0))
    project(block(3, 0))
    start(direct, 0)
    start(direct, 1)
    for i in (block(0, 0), block(2, 2), block(1, 2), block(3, 2), block(0, 2)):
        project(i)
    pass_on(0)
    pass_on(1)
    zsend[0] = arrived(0)
    z_copy(0).start()
    start(transit, 2)
    zsend[1] = arrived(1)
    z_copy(1).start()
    start(transit, 3)
    start(direct, 2)
    start(direct, 3)
    pass_on(2)
    pass_on(3)
    for p in range(2):
        here = arrived(2 + p)
        z_copy(p).wait()
        own_rows[p * size : (p + 1) * size] = here + zrecv[p]
    own = own_rows[...]

    PG[v] = jnp.transpose(own).astype(BF16)

    def gather_own(k):
        return send(PG.at[v], PG.at[v], y_ssem.at[24 + k], y_rsem.at[24 + k], peer(dy=k))

    def gather_other(k):
        return send(PG.at[vz], PG.at[vz], y_ssem.at[28 + k], y_rsem.at[28 + k], peer(dy=k))

    gather_z = send(PG.at[v], PG.at[v], z_ssem.at[2], z_rsem.at[2], peer(dzh=1))
    gather_z.start()

    gram = lax.dot_general(own, own, (((0,), (0,)), ((), ())), precision=HIGHEST, preferred_element_type=F32)
    gbuf[...] = (gram / count).reshape(gbuf.shape)
    g_core = send(gbuf.at[1 - c], grecv, c_ssem.at[2], c_rsem.at[2], peer(dc=1))
    g_core.start()
    for k in order:
        gather_own(k).start()
    g_core.wait()
    gbuf[c] = gbuf[c] + grecv[...]
    gxy[xy] = gbuf[c, xy]

    def gram_scatter(k):
        to = ((x + k // 4) % NX) * NY + (y + k % 4) % NY
        return send(gbuf.at[c, to], gxy.at[xy], g_ssem.at[k], g_rsem.at[k], peer(dx=k // 4, dy=k % 4))

    def gram_z(k):
        return send(gz.at[z], gz.at[z], g_ssem.at[16 + k], g_rsem.at[16 + k], peer(dzh=k // 4, dzl=k % 4))

    def gram_gather(k):
        return send(gfin.at[c, xy], gfin.at[c, xy], g_ssem.at[24 + k], g_rsem.at[24 + k], peer(dx=k // 4, dy=k % 4))

    loop(1, 16, lambda k: gram_scatter(k).start())
    loop(1, 16, lambda k: gram_scatter(k).wait())
    gz[z] = jnp.sum(gxy[...], axis=0)
    loop(1, 8, lambda k: gram_z(k).start())
    gather_z.wait()
    for k in order:
        gather_other(k).start()


    loop(1, 8, lambda k: gram_z(k).wait())
    gfin[c, xy] = jnp.sum(gz[...], axis=0)
    loop(1, 16, lambda k: gram_gather(k).start())

    loop(1, 4, lambda k: gather_own(k).wait())

    def products(j, which):
        at = pl.ds(pl.multiple_of(j * 256, 256), 256)
        acc = jnp.zeros((256, 256), F32)
        for i in which:
            acc = acc + jnp.dot(PG[i], X[i, :, at], preferred_element_type=F32)
        return acc.reshape(2, 128, 256)

    def first_product(j):
        TT[j] = products(j, [q * NZH + zh for q in range(NY)] + [vz])

    loop(0, 8, first_product)

    loop(1, 4, lambda k: gather_other(k).wait())
    total = jnp.zeros((256, 128), F32)
    for i in range(8):
        part = PG[i].astype(F32)
        total = total + (part[:, :128] + part[:, 128:])
    total = jnp.sum(total, axis=1, keepdims=True).reshape(2, 128, 1)
    root = math.sqrt(count)

    def t_core(j):
        return send(TT.at[j, 1 - c], trecv.at[j], tc_ssem.at[j], tc_rsem.at[j], peer(dc=1))

    def second_product(j):
        acc = TT[j] + products(j, [((y + k) % NY) * NZH + 1 - zh for k in order])
        mean = jnp.concatenate([st[pl.ds(2 * j, 1), :], st[pl.ds(2 * j + 1, 1), :]], axis=1)
        inv_sd = jnp.concatenate([st[pl.ds(16 + 2 * j, 1), :], st[pl.ds(17 + 2 * j, 1), :]], axis=1)
        TT[j] = (inv_sd / root) * (acc - total * mean)
        t_core(j).start()

    for k in order + (0,):
        first = ((x + k) % NX) * 2
        loop(0, 2, lambda q: second_product(first + q))

    def t_x(k, h):
        to = ((x + k) % NX) * 2
        at = pl.ds(h * 64, 64)
        i = 4 * h + k
        return send(TM.at[pl.ds(to, 2), at], tx.at[x, :, at], t_ssem.at[i], t_rsem.at[i], peer(dx=k))

    def t_z(k, h):
        i = 8 + 4 * h + k
        return send(TX.at[h, (zl + k) % NZL], tz.at[h, zl], t_ssem.at[i], t_rsem.at[i], peer(dzl=k))

    def merge_x(h):
        for k in order:
            t_x(k, h).wait()
        at = pl.ds(h * 64, 64)
        acc = TM[pl.ds(2 * x, 2), at]
        for k in order:
            acc = acc + tx[(x + k) % NX, :, at]
        for q in range(NZL):
            TX[h, q] = acc[q // 2, :, q % 2 * 128 : q % 2 * 128 + 128]
        for k in order:
            t_z(k, h).start()

    for k in order + (0,):
        for q in range(2):
            j = ((x + k) % NX) * 2 + q
            t_core(j).wait()
            TM[j] = TT[j, c] + trecv[j]
        if k:
            t_x(k, 0).start()
    for k in order:
        t_x(k, 1).start()

    loop(1, 16, lambda k: gram_gather(k).wait())
    g_back = send(gfin.at[c], gfin.at[c], c_ssem.at[3], c_rsem.at[3], peer(dc=1))
    g_back.start()
    g_back.wait()
    n = own.shape[1]
    M[:, :n] = gfin[...].reshape(n, n)
    M[:, n:] = (iota((n, n), 0) == iota((n, n), 1)).astype(F32)

    factor_rows(M, Y, 0)
    merge_x(0)
    factor_rows(M, Y, 1)
    factor_rows(M, Y, 2)
    merge_x(1)
    factor_rows(M, Y, 3)
    basis_ref[...] = lax.dot_general(
        own_rows[...], M[:, n:], (((1,), (1,)), ((), ())), precision=HIGHEST, preferred_element_type=F32
    )
    mine = pl.ds(pl.multiple_of(c * 128, 128), 128)
    for h in range(2):
        for k in order:
            t_z(k, h).wait()
        acc = TX[h, zl]
        for k in order:
            acc = acc + tz[h, (zl + k) % NZL]
        tfin[pl.ds(pl.multiple_of(c * 128 + h * 64, 64), 64)] = acc
    t_back = send(tfin.at[mine], tfin.at[mine], c_ssem.at[5], c_rsem.at[5], peer(dc=1))
    t_back.start()
    t_back.wait()
    loads = jnp.transpose(jnp.dot(M[:, n:], tfin[...], precision=HIGHEST, preferred_element_type=F32))
    load_ref[...] = jnp.where(c == 0, loads[:64], loads[64:])


def power_step(dosage, sketch, count):
    rows, cols = dosage.shape
    k = sketch.shape[1]
    vm = pltpu.VMEM
    dma = pltpu.SemaphoreType.DMA
    vmem = pl.BlockSpec(memory_space=pltpu.VMEM)
    return pl.pallas_call(
        functools.partial(comm_kernel, count),
        out_shape=(
            jax.ShapeDtypeStruct((rows // 8, k), F32),
            jax.ShapeDtypeStruct((64, k), F32),
        ),
        in_specs=[pl.BlockSpec(memory_space=pl.ANY), vmem],
        out_specs=(vmem, vmem),
        scratch_shapes=[
            vm((8, rows // 8, cols), BF16),
            vm((16, 2, 64, k), BF16),
            vm((cols, k), BF16),
            vm((32, 128), F32),
            vm((32, 128), F32),
            vm((4, 32, 128), F32),
            vm((4, 32, 128), F32),
            vm((8, rows // 8, k), F32),
            vm((4, 2, rows // 32, k), F32),
            vm((4, 2, rows // 32, k), F32),
            vm((4, 2, rows // 32, k), F32),
            vm((2, rows // 16, k), F32),
            vm((2, rows // 16, k), F32),
            vm((8, k, rows // 8), BF16),
            vm((8, 2, k // 2, cols // 8), F32),
            vm((8, k // 2, cols // 8), F32),
            vm((8, k // 2, cols // 8), F32),
            vm((4, 2, k // 2, cols // 8), F32),
            vm((2, 4, k // 4, 128), F32),
            vm((2, 4, k // 4, 128), F32),
            vm((k, 128), F32),
            vm((2, 16, 8, k), F32),
            vm((16, 8, k), F32),
            vm((16, 8, k), F32),
            vm((8, 8, k), F32),
            vm((2, 16, 8, k), F32),
            vm((k, 2 * k), F32),
            vm((NB, 2 * NB), F32),
            vm((rows // 8, k), F32),
            dma((8,)),
            dma((6,)), dma((6,)),
            dma((20,)), dma((20,)),
            dma((4,)), dma((4,)),
            dma((8,)), dma((8,)),
            dma((32,)), dma((32,)),
            dma((3,)), dma((3,)),
            dma((40,)), dma((40,)),
            dma((16,)), dma((16,)),
            dma((8,)), dma((8,)),
        ],
        compiler_params=pltpu.CompilerParams(
            collective_id=0, has_side_effects=True, vmem_limit_bytes=56 * 2**20
        ),
        name="power_step",
    )(dosage, sketch)


def local(dosage, sketch):
    count = dosage.shape[0] * lax.axis_size("samples")
    return power_step(dosage, sketch, count)


def solution(mesh):
    in_specs = (P("samples", "variants"), P(("variants", "samples"), None))
    out_specs = (P(("samples", "variants"), None), P(("variants", "samples"), None))
    return jax.shard_map(local, mesh=mesh, in_specs=in_specs, out_specs=out_specs, check_vma=False)
```

time: 137 us -> 102 us (0.74)
  Pallas kernels: 133 us -> 98.1 us
    pallas_call x2 -> x1, Pallas kernels: 133 us -> 98.1 us  [power_step(): pl.pallas_call(functools.partial(comm_kernel, count), out_shape=(jax.Shap...]
    unnamed x6 -> x2, local copies, waits for them, and re-layouts: 2.8 us -> 3.14 us
where the time goes in v2:
time: 102 us
  Pallas kernels  98.1 us (96%)
  local copies, waits for them, and re-layouts  3.14 us (3%)
    pallas_call x1, Pallas kernels, power_step(): pl.pallas_call(functools.partial(comm_kernel, count), out_shape=(jax.Shap...  98.1 us
    unnamed x2, local copies, waits for them, and re-layouts  3.14 us

profile of v2, /device:TPU:1, one launch (start us, length us, event | category | flops | bytes accessed | tf_op | source)
XLA Modules:
  0.0 101.9 jit_solution(17959353442621376733)
XLA Ops:
  0.6 98.1 %power_step.1 = (f32[256,256]{1,0:T(8,128)}, f32[64,256]{1,0:T(8,128)}) custom-call(bf16[2048,2048]{1,0:T(8,128)(2,1)} %x_hbm.1, bf16[64,256]{1,0:T(8,128)(2,1)} %sk_ref.1), custom_call_target="tpu_custom_call" | custom-call | tf_op jit(solution)/shard_map/power_step/pallas_call | solution.py:497
  98.8 1.7 %copy.6 = f32[256,256]{1,0:T(8,128)} copy(f32[256,256]{1,0:T(8,128)} %get-tuple-element.4) | data formatting | bytes 524288
  100.4 1.5 %copy.7 = f32[64,256]{1,0:T(8,128)} copy(f32[64,256]{1,0:T(8,128)} %get-tuple-element.5) | data formatting | bytes 131072

commit v3 on v2

--- a/solution.py
+++ b/solution.py
@@ -86,12 +86,18 @@
     at = slice(b * NB, (b + 1) * NB)
     eye = (iota((NB, NB), 0) == iota((NB, NB), 1)).astype(F32)
     factor_diagonal(jnp.concatenate([M[at, at], eye], axis=1), Y)
-    panel = jnp.dot(Y[:, NB:], M[at, :], precision=HIGHEST, preferred_element_type=F32)
-    M[at, :] = panel
+    first = b * NB // 128 * 128
+    last = n + -(-(b + 1) * NB // 128) * 128
+    panel = jnp.dot(Y[:, NB:], M[at, first:last], precision=HIGHEST, preferred_element_type=F32)
+    M[at, first:last] = panel
     if (b + 1) * NB < n:
         rest = slice((b + 1) * NB, n)
-        M[rest, :] = M[rest, :] - lax.dot_general(
-            panel[:, rest], panel, (((0,), (0,)), ((), ())), precision=HIGHEST, preferred_element_type=F32
+        M[rest, first:last] = M[rest, first:last] - lax.dot_general(
+            panel[:, (b + 1) * NB - first : n - first],
+            panel,
+            (((0,), (0,)), ((), ())),
+            precision=HIGHEST,
+            preferred_element_type=F32,
         )
 
 
@@ -320,12 +326,10 @@
     project(block(2, 0))
     start(transit, 0)
     start(transit, 1)
-    project(block(1, 0))
-    project(block(3, 0))
+    loop(0, 2, lambda q: project(block(1 + 2 * q, 0)))
     start(direct, 0)
     start(direct, 1)
-    for i in (block(0, 0), block(2, 2), block(1, 2), block(3, 2), block(0, 2)):
-        project(i)
+    loop(0, 5, lambda q: project(((y + q) % NY) * NZH + zh + (4 - q) // 4 * (1 - 2 * zh)))
     pass_on(0)
     pass_on(1)
     zsend[0] = arrived(0)
@@ -359,8 +363,6 @@
     gbuf[...] = (gram / count).reshape(gbuf.shape)
     g_core = send(gbuf.at[1 - c], grecv, c_ssem.at[2], c_rsem.at[2], peer(dc=1))
     g_core.start()
-    for k in order:
-        gather_own(k).start()
     g_core.wait()
     gbuf[c] = gbuf[c] + grecv[...]
     gxy[xy] = gbuf[c, xy]
@@ -376,12 +378,14 @@
         return send(gfin.at[c, xy], gfin.at[c, xy], g_ssem.at[24 + k], g_rsem.at[24 + k], peer(dx=k // 4, dy=k % 4))
 
     loop(1, 16, lambda k: gram_scatter(k).start())
+    for k in order:
+        gather_own(k).start()
+    gather_z.wait()
+    for k in order:
+        gather_other(k).start()
     loop(1, 16, lambda k: gram_scatter(k).wait())
     gz[z] = jnp.sum(gxy[...], axis=0)
     loop(1, 8, lambda k: gram_z(k).start())
-    gather_z.wait()
-    for k in order:
-        gather_other(k).start()
 
 
     loop(1, 8, lambda k: gram_z(k).wait())
@@ -465,8 +469,8 @@
     M[:, n:] = (iota((n, n), 0) == iota((n, n), 1)).astype(F32)
 
     factor_rows(M, Y, 0)
+    factor_rows(M, Y, 1)
     merge_x(0)
-    factor_rows(M, Y, 1)
     factor_rows(M, Y, 2)
     merge_x(1)
     factor_rows(M, Y, 3)
@@ -497,8 +501,8 @@
     return pl.pallas_call(
         functools.partial(comm_kernel, count),
         out_shape=(
-            jax.ShapeDtypeStruct((rows // 8, k), F32),
-            jax.ShapeDtypeStruct((64, k), F32),
+            pltpu.VMEM((rows // 8, k), F32),
+            pltpu.VMEM((64, k), F32),
         ),
         in_specs=[pl.BlockSpec(memory_space=pl.ANY), vmem],
         out_specs=(vmem, vmem),
@@ -550,9 +554,33 @@
     )(dosage, sketch)
 
 
+def store_kernel(basis_ref, load_ref, basis_out, load_out, sem):
+    copies = [
+        pltpu.make_async_copy(basis_ref, basis_out, sem.at[0]),
+        pltpu.make_async_copy(load_ref, load_out, sem.at[1]),
+    ]
+    for copy in copies:
+        copy.start()
+    for copy in copies:
+        copy.wait()
+
+
+def store(basis, loadings):
+    vmem = pl.BlockSpec(memory_space=pltpu.VMEM)
+    hbm = pl.BlockSpec(memory_space=pltpu.HBM)
+    return pl.pallas_call(
+        store_kernel,
+        out_shape=(jax.ShapeDtypeStruct(basis.shape, F32), jax.ShapeDtypeStruct(loadings.shape, F32)),
+        in_specs=[vmem, vmem],
+        out_specs=(hbm, hbm),
+        scratch_shapes=[pltpu.SemaphoreType.DMA((2,))],
+        name="store",
+    )(basis, loadings)
+
+
 def local(dosage, sketch):
     count = dosage.shape[0] * lax.axis_size("samples")
-    return power_step(dosage, sketch, count)
+    return store(*power_step(dosage, sketch, count))
 
 
 def solution(mesh):

time: 102 us -> 99.2 us (0.973)
  local copies, waits for them, and re-layouts: 3.14 us -> 1.31 us
  Pallas kernels: 98.1 us -> 96.9 us
    unnamed x2 -> x4, local copies, waits for them, and re-layouts: 3.14 us -> 1.31 us
    pallas_call x1 -> x2, Pallas kernels: 98.1 us -> 96.9 us  [the longest x1 95.2 us: power_step(): pl.pallas_call(functools.partial(comm_kernel, count), out_shape=(pltpu.VM...]
where the time goes in v3:
time: 99.2 us; the launch traced here: 99 us
  Pallas kernels  96.9 us (98%)
  local copies, waits for them, and re-layouts  1.31 us (1%)
    pallas_call x1, Pallas kernels, power_step(): pl.pallas_call(functools.partial(comm_kernel, count), out_shape=(pltpu.VM...  95.2 us

profile of v3, /device:TPU:1, one launch (start us, length us, event | category | flops | bytes accessed | tf_op | source)
XLA Modules:
  0.0 99.0 jit_solution(3544707984388249785)
XLA Ops:
  0.6 95.2 %power_step.1 = (f32[256,256]{1,0:T(8,128)S(1)}, f32[64,256]{1,0:T(8,128)S(1)}) custom-call(bf16[2048,2048]{1,0:T(8,128)(2,1)} %x_hbm.1, bf16[64,256]{1,0:T(8,128)(2,1)} %sk_ref.1), custom_call_target="tpu_custom_call" | custom-call | tf_op jit(solution)/shard_map/power_step/pallas_call | solution.py:501
  95.9 0.0 copy-start
  95.9 0.7 copy-done
  96.6 0.0 copy-start.1
  96.6 0.6 copy-done.1
  97.2 1.7 %store.1 = (f32[256,256]{1,0:T(8,128)}, f32[64,256]{1,0:T(8,128)}) custom-call(f32[256,256]{1,0:T(8,128)} %copy-done, f32[64,256]{1,0:T(8,128)} %copy-done.1), custom_call_target="tpu_custom_call" | custom-call | tf_op jit(solution)/shard_map/store/pallas_call | solution.py:571
Async XLA Ops:
  95.9 0.7 copy-start
  96.6 0.6 copy-start.1

commit v4 on v3

--- a/solution.py
+++ b/solution.py
@@ -102,7 +102,7 @@
 
 
 def comm_kernel(
-    count, x_hbm, sk_ref, basis_ref, load_ref,
+    count, x_hbm, sk_hbm, basis_ref, load_ref,
     X, skbuf, W, st, st_c, st_x, st_z, Pp, tr, di, mg, zsend, zrecv,
     PG, TT, trecv, TM, tx, TX, tz, tfin, gbuf, grecv, gxy, gz, gfin, M, Y, own_rows,
     x_sem, c_ssem, c_rsem, sk_ssem, sk_rsem, fw_ssem, fw_rsem, st_ssem, st_rsem, y_ssem, y_rsem,
@@ -125,6 +125,7 @@
             src_ref=src, dst_ref=dst, send_sem=ssem, recv_sem=rsem, device_id=to, device_id_type=MESH
         )
 
+    load(0).start()
     barrier = pltpu.get_barrier_semaphore()
 
     def greet(to):
@@ -132,7 +133,9 @@
 
     loop(0, 4, lambda k: greet(peer(dzl=k, dzh=1)))
     loop(0, 9, lambda k: greet(peer(dx=k // 3 + 1, dy=k % 3 + 1)))
-    loop(0, blocks, lambda i: load(i).start())
+    sketch_in = pltpu.make_async_copy(sk_hbm, skbuf.at[xz, c], x_sem.at[blocks])
+    sketch_in.start()
+    loop(1, blocks, lambda i: load(i).start())
     loop(1, 4, lambda k: greet(peer(dzl=k)))
     loop(1, 4, lambda k: greet(peer(dx=k)))
     loop(1, 4, lambda k: greet(peer(dy=k)))
@@ -181,10 +184,10 @@
     pl.semaphore_wait(barrier, 23)
 
     def sketch_x(k):
-        return send(sk_ref, skbuf.at[xz, c], sk_ssem.at[k], sk_rsem.at[k], peer(dx=k))
+        return send(skbuf.at[xz, c], skbuf.at[xz, c], sk_ssem.at[k], sk_rsem.at[k], peer(dx=k))
 
     def sketch_z(k):
-        return send(sk_ref, skbuf.at[xz, c], sk_ssem.at[4 + k], sk_rsem.at[4 + k], peer(dzl=k))
+        return send(skbuf.at[xz, c], skbuf.at[xz, c], sk_ssem.at[4 + k], sk_rsem.at[4 + k], peer(dzl=k))
 
     def sketch_zx(j, k):
         at = x * NZL + (zl + NZL - j) % NZL
@@ -195,11 +198,11 @@
         at = pl.ds(((x + k) % NX) * NZL, NZL)
         return send(skbuf.at[at, c], skbuf.at[at, c], fw_ssem.at[k], fw_rsem.at[k], peer(dc=1))
 
+    sketch_in.wait()
     for k in order:
         sketch_z(k).start()
     for k in order:
         sketch_x(k).start()
-    skbuf[xz, c] = sk_ref[...]
 
     sums = lax.fori_loop(early, blocks, block_sums, sums)
 
@@ -334,9 +337,9 @@
     pass_on(1)
     zsend[0] = arrived(0)
     z_copy(0).start()
-    start(transit, 2)
     zsend[1] = arrived(1)
     z_copy(1).start()
+    start(transit, 2)
     start(transit, 3)
     start(direct, 2)
     start(direct, 3)
@@ -504,7 +507,7 @@
             pltpu.VMEM((rows // 8, k), F32),
             pltpu.VMEM((64, k), F32),
         ),
-        in_specs=[pl.BlockSpec(memory_space=pl.ANY), vmem],
+        in_specs=[pl.BlockSpec(memory_space=pl.ANY), pl.BlockSpec(memory_space=pl.ANY)],
         out_specs=(vmem, vmem),
         scratch_shapes=[
             vm((8, rows // 8, cols), BF16),
@@ -536,7 +539,7 @@
             vm((k, 2 * k), F32),
             vm((NB, 2 * NB), F32),
             vm((rows // 8, k), F32),
-            dma((8,)),
+            dma((9,)),
             dma((6,)), dma((6,)),
             dma((20,)), dma((20,)),
             dma((4,)), dma((4,)),

time: 99.2 us -> 98.7 us (level)
  no operation moved by 1% of the time
where the time goes in v4:
time: 98.7 us; the launch traced here: 98.6 us
  Pallas kernels  96.4 us (98%)
  local copies, waits for them, and re-layouts  1.31 us (1%)
    pallas_call x1, Pallas kernels, power_step(): pl.pallas_call(functools.partial(comm_kernel, count), out_shape=(pltpu.VM...  94.8 us

profile of v4, /device:TPU:1, one launch (start us, length us, event | category | flops | bytes accessed | tf_op | source)
XLA Modules:
  0.0 98.6 jit_solution(3859042793444113312)
XLA Ops:
  0.6 94.8 %power_step.1 = (f32[256,256]{1,0:T(8,128)S(1)}, f32[64,256]{1,0:T(8,128)S(1)}) custom-call(bf16[2048,2048]{1,0:T(8,128)(2,1)} %x_hbm.1, bf16[64,256]{1,0:T(8,128)(2,1)} %sk_hbm.1), custom_call_target="tpu_custom_call" | custom-call | tf_op jit(solution)/shard_map/power_step/pallas_call | solution.py:504
  95.4 0.0 copy-start
  95.4 0.7 copy-done
  96.1 0.0 copy-start.1
  96.1 0.6 copy-done.1
  96.7 1.7 %store.1 = (f32[256,256]{1,0:T(8,128)}, f32[64,256]{1,0:T(8,128)}) custom-call(f32[256,256]{1,0:T(8,128)} %copy-done, f32[64,256]{1,0:T(8,128)} %copy-done.1), custom_call_target="tpu_custom_call" | custom-call | tf_op jit(solution)/shard_map/store/pallas_call | solution.py:574
Async XLA Ops:
  95.4 0.7 copy-start
  96.1 0.6 copy-start.1
